TPU v7x, 512 devices: a whole 4x4x16 slice. The times are simulated.
512 devices in a mesh: pm: 2 (over y_lo), ka: 128 (over x, z, core), isdf: 2 (over y_hi).
Axes of the slice: x: 4, y: 4 (y_hi: 2, y_lo: 2; y = y_hi * 2 + y_lo), z: 16, core: 2. Of those that a mesh axis runs over, the one named last changes fastest.
Arguments:
- amplitudes: bfloat16 [2, 2, 2, 256, 64, 256], P('pm', None, None, 'ka'), may hold values from -6 to 6
- conduction: bfloat16 [2, 256, 256, 512], P(None, 'ka', None, 'isdf'), may hold values from -0.375 to 0.375
- valence: bfloat16 [2, 256, 64, 512], P(None, 'ka'), may hold values from -0.75 to 0.75
- energy: float32 [256, 64, 256], P('ka', None, 'isdf'), may hold values from 0.5 to 2.5
- screened: bfloat16 [4, 2, 512, 512], P(None, None, 'isdf'), may hold values from -0.59765625 to 0.59765625
- coulomb: float32 [512, 512], P(None, 'isdf'), may hold values from -0.03125 to 0.03125
- mirror: int32 [256], P('ka'), may hold values from 0 to 255, as said below
- transfer_class: int32 [256, 256], P('ka'), may hold values from 0 to 3, as said below
Outputs:
- response: bfloat16 [2, 2, 2, 256, 64, 256], P('pm', None, None, 'ka', None, 'isdf')
Inputs may be any that keep to these rules, and one draw needn't show every extreme that they name: mirror[mirror[k]] = k; a k-point of block j (the aligned block of 2 k-points that holds it) has its mirror in block 127 - j. transfer_class[k, k2] depends only on (k - k2) mod 256.
All inputs are finite; a program needn't handle non-finite values.
Results may differ from a plain program's by a relative error of at most 0.015.
Values may be sent and summed in bfloat16 or wider, within the bound.
A program may use at most 128 MiB of HBM per device.

v0:
```python
import jax
import jax.numpy as jnp
from jax import lax
from jax.sharding import PartitionSpec as P

REACH = 2
HIGHEST = lax.Precision.HIGHEST


def swapped(block, axis, apart):
    count = lax.axis_size(axis)
    route = []
    for low in range(count):
        high = low | 1 << apart
        if high != low and high < count:
            route += [(low, high), (high, low)]
    return lax.ppermute(block, axis, route)


def shifted(value, axis, by):
    size = lax.axis_size(axis)
    return lax.ppermute(value, axis, [(i, (i + by) % size) for i in range(size)])


def pair_einsum(pattern, left, right, conjugate):

    def single(first, second):
        return jnp.einsum(pattern, first, second, preferred_element_type=jnp.float32)

    if conjugate:
        real_part = single(left[0], right[0]) + single(left[1], right[1])
        imag_part = single(left[1], right[0]) - single(left[0], right[1])
    else:
        real_part = single(left[0], right[0]) - single(left[1], right[1])
        imag_part = single(left[0], right[1]) + single(left[1], right[0])
    return (real_part, imag_part)


def conjugated(field):
    return jnp.stack([field[:, 0], -field[:, 1]], axis=1)


def coefficients(vector, conduction):
    real_part, imag_part = pair_einsum(
        "bkvc,kcm->bkvm", (vector[:, 0], vector[:, 1]), (conduction[0], conduction[1]), False
    )
    return jnp.stack([real_part, imag_part], axis=1).astype(jnp.bfloat16)


def amp_bits(field):
    for bit_number in range(lax.axis_size("ka").bit_length() - 1):
        field = swapped(field, "ka", bit_number)
    return field


def result_bits(field):
    for bit_number in range(lax.axis_size("ka").bit_length() - 1):
        field = swapped(field, "ka", bit_number)
    return field


def per_device(amplitudes, conduction, valence, energy, screened, coulomb, mirror, transfer_class):
    pm_index = lax.axis_index("pm")
    ka_index = lax.axis_index("ka")
    isdf_index = lax.axis_index("isdf")
    ka_count = lax.axis_size("ka")
    kpoint_count = conduction.shape[1]
    mu_count = conduction.shape[3]
    point_count = valence.shape[3]
    cond_share = energy.shape[2]
    vector_count = amplitudes.shape[1]
    is_plus = pm_index == 0
    parity = jnp.where(is_plus, 1.0, -1.0).astype(jnp.float32)
    exchange_weight = jnp.where(is_plus, 4.0, 0.0).astype(jnp.float32)
    local_amps = amplitudes[0]
    partner_amps = swapped(local_amps, "pm", 0)
    partner_side = jnp.where(is_plus, partner_amps, local_amps)
    distant_side = amp_bits(partner_side)
    direct = jnp.where(is_plus, local_amps, partner_amps).astype(jnp.float32)
    local_mirror = mirror - (ka_count - 1 - ka_index) * kpoint_count
    flipped = conjugated(jnp.take(distant_side, local_mirror, axis=2).astype(jnp.float32))
    vector = (direct + parity * flipped).astype(jnp.bfloat16)
    own_coef = coefficients(vector, conduction)
    valence_part = lax.dynamic_slice_in_dim(valence, isdf_index * mu_count, mu_count, 3)
    rho_real = jnp.einsum(
        "kvm,bkvm->bm", valence_part[0], own_coef[:, 0], preferred_element_type=jnp.float32
    )
    rho_real = rho_real + jnp.einsum(
        "kvm,bkvm->bm", valence_part[1], own_coef[:, 1], preferred_element_type=jnp.float32
    )
    rho_imag = jnp.einsum(
        "kvm,bkvm->bm", valence_part[0], own_coef[:, 1], preferred_element_type=jnp.float32
    )
    rho_imag = rho_imag - jnp.einsum(
        "kvm,bkvm->bm", valence_part[1], own_coef[:, 0], preferred_element_type=jnp.float32
    )
    density = jnp.stack([rho_real, rho_imag], axis=1)
    spread = jnp.einsum("nm,brm->brn", coulomb, density, precision=HIGHEST)
    spread = lax.psum(spread, ("ka", "isdf"))
    potential = lax.dynamic_slice_in_dim(spread, isdf_index * mu_count, mu_count, 2)
    class_ids = jnp.arange(screened.shape[0], dtype=jnp.int32)

    def accumulate(totals, coef_block, valence_block, source):
        pair_real, pair_imag = pair_einsum(
            "bqvm,qvn->bqmn",
            (coef_block[:, 0], coef_block[:, 1]),
            (valence_block[0], valence_block[1]),
            True,
        )
        pair_real = pair_real.astype(jnp.bfloat16)
        pair_imag = pair_imag.astype(jnp.bfloat16)
        classes = lax.dynamic_slice_in_dim(transfer_class, source * kpoint_count, kpoint_count, 1)
        selector = (classes[:, :, None] == class_ids).astype(jnp.bfloat16)
        total_real, total_imag = totals
        for visitor in range(kpoint_count):
            chosen = jnp.einsum(
                "kw,wrmn->rkmn", selector[:, visitor], screened, preferred_element_type=jnp.float32
            ).astype(jnp.bfloat16)
            screen_real = chosen[0][None].astype(jnp.float32)
            screen_imag = chosen[1][None].astype(jnp.float32)
            visit_real = pair_real[:, visitor][:, None].astype(jnp.float32)
            visit_imag = pair_imag[:, visitor][:, None].astype(jnp.float32)
            total_real = total_real + (screen_real * visit_real - screen_imag * visit_imag)
            total_imag = total_imag + (screen_real * visit_imag + screen_imag * visit_real)
        return (total_real, total_imag)

    payload = (vector, conduction, valence)

    def advance(moving, offset):
        return shifted((moving[0], moving[1], moving[2]), "ka", offset)

    def unpack(moving):
        return (coefficients(moving[0], moving[1]), moving[2])

    def visit(totals, moving, distance):
        coef_block, valence_block = unpack(moving)
        source = jnp.mod(ka_index + distance, ka_count)
        return accumulate(totals, coef_block, valence_block, source)

    zero_field = jnp.zeros((vector_count, kpoint_count, mu_count, point_count), jnp.float32)
    totals = accumulate((zero_field, zero_field), own_coef, valence, ka_index)
    below_item = payload
    for count_done in range(REACH):
        below_item = advance(below_item, 1)
        totals = visit(totals, below_item, -(count_done + 1))
    above_item = payload
    for count_done in range(REACH):
        above_item = advance(above_item, -1)
        totals = visit(totals, above_item, count_done + 1)
    sum_real = totals[0].astype(jnp.bfloat16)
    sum_imag = totals[1].astype(jnp.bfloat16)
    back_real, back_imag = pair_einsum(
        "bkmn,kvn->bkvm", (sum_real, sum_imag), (valence[0], valence[1]), False
    )
    potential_real = potential[:, 0][:, None, None, :]
    potential_imag = potential[:, 1][:, None, None, :]
    exchange_real = potential_real * valence_part[0] - potential_imag * valence_part[1]
    exchange_imag = potential_real * valence_part[1] + potential_imag * valence_part[0]
    field_real = (exchange_weight * exchange_real - back_real).astype(jnp.bfloat16)
    field_imag = (exchange_weight * exchange_imag - back_imag).astype(jnp.bfloat16)
    out_real, out_imag = pair_einsum(
        "bkvm,kcm->bkvc", (field_real, field_imag), (conduction[0], conduction[1]), True
    )
    partial_out = jnp.stack([out_real, out_imag], axis=1)
    summed = lax.psum_scatter(
        partial_out.astype(jnp.bfloat16), "isdf", scatter_dimension=4, tiled=True
    ).astype(jnp.float32)
    vector_part = lax.dynamic_slice_in_dim(vector, isdf_index * cond_share, cond_share, 4).astype(
        jnp.float32
    )
    channel_out = (energy[None, None] * vector_part + summed).astype(jnp.bfloat16)
    partner_out = swapped(channel_out, "pm", 0)
    blended = (
        0.5 * (partner_out.astype(jnp.float32) + parity * channel_out.astype(jnp.float32))
    ).astype(jnp.bfloat16)
    distant_out = result_bits(blended)
    reflected = conjugated(jnp.take(distant_out, local_mirror, axis=2))
    result = jnp.where(is_plus, blended, reflected)
    return result[None]


def solution(mesh):
    return jax.shard_map(
        per_device,
        mesh=mesh,
        in_specs=(
            P("pm", None, None, "ka", None, None),
            P(None, "ka", None, "isdf"),
            P(None, "ka", None, None),
            P("ka", None, "isdf"),
            P(None, None, "isdf", None),
            P(None, "isdf"),
            P("ka"),
            P("ka", None),
        ),
        out_specs=P("pm", None, None, "ka", None, "isdf"),
        check_vma=False,
    )
```

profile of v0, /device:TPU:2, one launch (start us, length us, event | category | flops | bytes accessed | tf_op | source)
XLA Modules:
  0.0 1090.2 jit_solution(7875653439164302398)
XLA Ops:
  8.6 10.8 collective-permute-start.15
  21.3 5.8 collective-permute-start.16
  76.7 6.6 collective-permute-done.2
  87.2 12.3 %collective-permute-done.3 = bf16[2,2,2,64,256]{4,3,0,2,1:T(8,128)(2,1)S(1)} collective-permute-done((bf16[2,2,2,64,256]{4,3,0,2,1:T(8,128)(2,1)S(1)}, bf16[2,2,2,64,256]{4,3,0,2,1:T(8,128)(2,1)S(1)}, u32[]{:S(2)}, u32[]{:S(2)}) %collective-permute-start.3) | collective-permute-done | bytes 262176 | tf_op jit(solution)/shard_map/ppermute | solution.py:17
  104.0 22.7 %collective-permute-done.4 = bf16[2,2,2,64,256]{4,3,0,2,1:T(8,128)(2,1)S(1)} collective-permute-done((bf16[2,2,2,64,256]{4,3,0,2,1:T(8,128)(2,1)S(1)}, bf16[2,2,2,64,256]{4,3,0,2,1:T(8,128)(2,1)S(1)}, u32[]{:S(2)}, u32[]{:S(2)}) %collective-permute-start.4) | collective-permute-done | bytes 262176 | tf_op jit(solution)/shard_map/ppermute | solution.py:17
  126.6 14.7 %collective-permute-start.5 = (bf16[2,2,2,64,256]{4,3,0,2,1:T(8,128)(2,1)S(1)}, bf16[2,2,2,64,256]{4,3,0,2,1:T(8,128)(2,1)S(1)}, u32[]{:S(2)}, u32[]{:S(2)}) collective-permute-start(bf16[2,2,2,64,256]{4,3,0,2,1:T(8,128)(2,1)S(1)} %collective-permute-done.4), channel_id=1, source_target_pairs={{0,32},{32,0},{2,34},{34,2},{4,36},{36,4},{6,38},{38,6},{8,40},{40... | collective-permute-start | bytes 786440 | tf_op jit(solution)/shard_map/ppermute | solution.py:17
  143.4 14.8 %collective-permute-done.5 = bf16[2,2,2,64,256]{4,3,0,2,1:T(8,128)(2,1)S(1)} collective-permute-done((bf16[2,2,2,64,256]{4,3,0,2,1:T(8,128)(2,1)S(1)}, bf16[2,2,2,64,256]{4,3,0,2,1:T(8,128)(2,1)S(1)}, u32[]{:S(2)}, u32[]{:S(2)}) %collective-permute-start.5) | collective-permute-done | bytes 262176 | tf_op jit(solution)/shard_map/ppermute | solution.py:17
  163.1 5.4 collective-permute-done.6
  198.8 5.8 collective-permute-start.19
  206.5 5.8 collective-permute-start.18
  228.5 583.0 %psum.7 = f32[2,2,512]{2,1,0:T(2,128)S(1)} all-reduce(f32[2,2,512]{2,1,0:T(2,128)S(1)} %fusion.90), channel_id=1, replica_groups=mesh['pm'=2,'ka'=128,'isdf'=2] {'ka','isdf'}, use_global_device_ids=true, to_apply=%region_0.1 | all-reduce | flops 2048 | bytes 16384 | tf_op jit(solution)/shard_map/psum | solution.py:99
  845.6 5.3 collective-permute-start.17
  878.6 9.2 add_convert_fusion
  887.9 9.5 add_convert_fusion.1
  901.8 92.5 %reduce-scatter.4.cloned.1.call-done = bf16[128,512]{1,0:T(8,128)(2,1)} async-done(((bf16[256,512]{1,0:T(8,128)(2,1)}), bf16[128,512]{1,0:T(8,128)(2,1)}) %reduce-scatter.4.cloned.1.call-update) | async-done | bytes 131088
  999.0 4.7 collective-permute-done.20
  1014.4 4.4 collective-permute-start.23
  1018.9 5.9 collective-permute-done.23
  1024.7 7.6 collective-permute-start.24
  1032.4 9.9 collective-permute-done.24
  1042.2 12.0 %collective-permute-start.25 = (bf16[2,2,2,64,128]{4,3,0,2,1:T(8,128)(2,1)S(1)}, bf16[2,2,2,64,128]{4,3,0,2,1:T(8,128)(2,1)S(1)}, u32[]{:S(2)}, u32[]{:S(2)}) collective-permute-start(bf16[2,2,2,64,128]{4,3,0,2,1:T(8,128)(2,1)S(1)} %collective-permute-done.24), channel_id=1, source_target_pairs={{0,32},{32,0},{2,34},{34,2},{4,36},{36,4},{6,38},{38,6},{8,40},{40... | collective-permute-start | bytes 393224 | tf_op jit(solution)/shard_map/ppermute | solution.py:17
  1054.2 12.1 %collective-permute-done.25 = bf16[2,2,2,64,128]{4,3,0,2,1:T(8,128)(2,1)S(1)} collective-permute-done((bf16[2,2,2,64,128]{4,3,0,2,1:T(8,128)(2,1)S(1)}, bf16[2,2,2,64,128]{4,3,0,2,1:T(8,128)(2,1)S(1)}, u32[]{:S(2)}, u32[]{:S(2)}) %collective-permute-start.25) | collective-permute-done | bytes 131104 | tf_op jit(solution)/shard_map/ppermute | solution.py:17
  1068.8 4.4 collective-permute-done.26
  1077.1 4.4 collective-permute-done.27
  (293 shorter events, 205.7 us)
Async XLA Ops:
  6.5 987.7 %reduce-scatter.4.cloned.1.call-start = ((), (), s32[]{:S(2)}) async-start(), calls=%async_computation.1 | async-start | bytes 393216
  6.5 198.1 %collective-permute-start.9 = (bf16[2,2,256,256]{3,2,1,0:T(8,128)(2,1)}, bf16[2,2,256,256]{3,2,1,0:T(8,128)(2,1)}, u32[]{:S(2)}, u32[]{:S(2)}) collective-permute-start(bf16[2,2,256,256]{3,2,1,0:T(8,128)(2,1)} %param.9), channel_id=1, source_target_pairs={{0,2},{2,4},{4,6},{6,8},{8,10},{10,12},{12,14},{14,16},{16,18},{18... | collective-permute-start | bytes 1572872 | tf_op jit(solution)/shard_map/ppermute | solution.py:22
  8.6 197.9 %collective-permute-start.15 = (bf16[2,2,256,256]{3,2,1,0:T(8,128)(2,1)}, bf16[2,2,256,256]{3,2,1,0:T(8,128)(2,1)}, u32[]{:S(2)}, u32[]{:S(2)}) collective-permute-start(bf16[2,2,256,256]{3,2,1,0:T(8,128)(2,1)} %param.9), channel_id=1, source_target_pairs={{0,254},{2,0},{4,2},{6,4},{8,6},{10,8},{12,10},{14,12},{16,14},{18... | collective-permute-start | bytes 1572872 | tf_op jit(solution)/shard_map/ppermute | solution.py:22
  19.4 177.4 %collective-permute-start.10 = (bf16[2,2,64,512]{3,2,1,0:T(8,128)(2,1)}, bf16[2,2,64,512]{3,2,1,0:T(8,128)(2,1)}, u32[]{:S(2)}, u32[]{:S(2)}) collective-permute-start(bf16[2,2,64,512]{3,2,1,0:T(8,128)(2,1)} %param.10), channel_id=1, source_target_pairs={{0,2},{2,4},{4,6},{6,8},{8,10},{10,12},{12,14},{14,16},{16,18},{18... | collective-permute-start | bytes 786440 | tf_op jit(solution)/shard_map/ppermute | solution.py:22
  21.3 177.5 %collective-permute-start.16 = (bf16[2,2,64,512]{3,2,1,0:T(8,128)(2,1)}, bf16[2,2,64,512]{3,2,1,0:T(8,128)(2,1)}, u32[]{:S(2)}, u32[]{:S(2)}) collective-permute-start(bf16[2,2,64,512]{3,2,1,0:T(8,128)(2,1)} %param.10), channel_id=1, source_target_pairs={{0,254},{2,0},{4,2},{6,4},{8,6},{10,8},{12,10},{14,12},{16,14},{18... | collective-permute-start | bytes 786440 | tf_op jit(solution)/shard_map/ppermute | solution.py:22
  28.1 40.2 %collective-permute-start = (bf16[2,2,2,64,256]{4,3,0,2,1:T(8,128)(2,1)S(1)}, bf16[2,2,2,64,256]{4,3,0,2,1:T(8,128)(2,1)S(1)}, u32[]{:S(2)}, u32[]{:S(2)}) collective-permute-start(bf16[2,2,2,64,256]{4,3,0,2,1:T(8,128)(2,1)S(1)} %bitcast.651), channel_id=1, source_target_pairs={{0,256},{256,0},{1,257},{257,1},{2,258},{258,2},{3,259},{259,3},{4... | collective-permute-start | bytes 786440 | tf_op jit(solution)/shard_map/ppermute | solution.py:17
  72.5 10.7 collective-permute-start.2
  83.2 16.3 %collective-permute-start.3 = (bf16[2,2,2,64,256]{4,3,0,2,1:T(8,128)(2,1)S(1)}, bf16[2,2,2,64,256]{4,3,0,2,1:T(8,128)(2,1)S(1)}, u32[]{:S(2)}, u32[]{:S(2)}) collective-permute-start(bf16[2,2,2,64,256]{4,3,0,2,1:T(8,128)(2,1)S(1)} %collective-permute-done.2), channel_id=1, source_target_pairs={{0,8},{8,0},{2,10},{10,2},{4,12},{12,4},{6,14},{14,6},{16,24},{24,... | collective-permute-start | bytes 786440 | tf_op jit(solution)/shard_map/ppermute | solution.py:17
  99.5 27.1 %collective-permute-start.4 = (bf16[2,2,2,64,256]{4,3,0,2,1:T(8,128)(2,1)S(1)}, bf16[2,2,2,64,256]{4,3,0,2,1:T(8,128)(2,1)S(1)}, u32[]{:S(2)}, u32[]{:S(2)}) collective-permute-start(bf16[2,2,2,64,256]{4,3,0,2,1:T(8,128)(2,1)S(1)} %collective-permute-done.3), channel_id=1, source_target_pairs={{0,16},{16,0},{2,18},{18,2},{4,20},{20,4},{6,22},{22,6},{8,24},{24... | collective-permute-start | bytes 786440 | tf_op jit(solution)/shard_map/ppermute | solution.py:17
  126.6 31.6 %collective-permute-start.5 = (bf16[2,2,2,64,256]{4,3,0,2,1:T(8,128)(2,1)S(1)}, bf16[2,2,2,64,256]{4,3,0,2,1:T(8,128)(2,1)S(1)}, u32[]{:S(2)}, u32[]{:S(2)}) collective-permute-start(bf16[2,2,2,64,256]{4,3,0,2,1:T(8,128)(2,1)S(1)} %collective-permute-done.4), channel_id=1, source_target_pairs={{0,32},{32,0},{2,34},{34,2},{4,36},{36,4},{6,38},{38,6},{8,40},{40... | collective-permute-start | bytes 786440 | tf_op jit(solution)/shard_map/ppermute | solution.py:17
  158.2 10.2 collective-permute-start.6
  168.4 43.9 %collective-permute-start.7 = (bf16[2,2,2,64,256]{4,3,0,2,1:T(8,128)(2,1)}, bf16[2,2,2,64,256]{4,3,0,2,1:T(8,128)(2,1)}, u32[]{:S(2)}, u32[]{:S(2)}) collective-permute-start(bf16[2,2,2,64,256]{4,3,0,2,1:T(8,128)(2,1)} %collective-permute-done.6), channel_id=1, source_target_pairs={{0,128},{128,0},{2,130},{130,2},{4,132},{132,4},{6,134},{134,6},{8... | collective-permute-start | bytes 786440 | tf_op jit(solution)/shard_map/ppermute | solution.py:17
  196.8 658.7 %collective-permute-start.13 = (bf16[2,2,64,512]{3,2,1,0:T(8,128)(2,1)}, bf16[2,2,64,512]{3,2,1,0:T(8,128)(2,1)}, u32[]{:S(2)}, u32[]{:S(2)}) collective-permute-start(bf16[2,2,64,512]{3,2,1,0:T(8,128)(2,1)} %collective-permute-done.10), channel_id=1, source_target_pairs={{0,2},{2,4},{4,6},{6,8},{8,10},{10,12},{12,14},{14,16},{16,18},{18... | collective-permute-start | bytes 786440 | tf_op jit(solution)/shard_map/ppermute | solution.py:22
  198.8 669.1 %collective-permute-start.19 = (bf16[2,2,64,512]{3,2,1,0:T(8,128)(2,1)}, bf16[2,2,64,512]{3,2,1,0:T(8,128)(2,1)}, u32[]{:S(2)}, u32[]{:S(2)}) collective-permute-start(bf16[2,2,64,512]{3,2,1,0:T(8,128)(2,1)} %collective-permute-done.16), channel_id=1, source_target_pairs={{0,254},{2,0},{4,2},{6,4},{8,6},{10,8},{12,10},{14,12},{16,14},{18... | collective-permute-start | bytes 786440 | tf_op jit(solution)/shard_map/ppermute | solution.py:22
  204.6 641.0 %collective-permute-start.12 = (bf16[2,2,256,256]{3,2,1,0:T(8,128)(2,1)}, bf16[2,2,256,256]{3,2,1,0:T(8,128)(2,1)}, u32[]{:S(2)}, u32[]{:S(2)}) collective-permute-start(bf16[2,2,256,256]{3,2,1,0:T(8,128)(2,1)} %collective-permute-done.9), channel_id=1, source_target_pairs={{0,2},{2,4},{4,6},{6,8},{8,10},{10,12},{12,14},{14,16},{16,18},{18... | collective-permute-start | bytes 1572872 | tf_op jit(solution)/shard_map/ppermute | solution.py:22
  206.5 656.7 %collective-permute-start.18 = (bf16[2,2,256,256]{3,2,1,0:T(8,128)(2,1)}, bf16[2,2,256,256]{3,2,1,0:T(8,128)(2,1)}, u32[]{:S(2)}, u32[]{:S(2)}) collective-permute-start(bf16[2,2,256,256]{3,2,1,0:T(8,128)(2,1)} %collective-permute-done.15), channel_id=1, source_target_pairs={{0,254},{2,0},{4,2},{6,4},{8,6},{10,8},{12,10},{14,12},{16,14},{18... | collective-permute-start | bytes 1572872 | tf_op jit(solution)/shard_map/ppermute | solution.py:22
  221.3 594.7 %collective-permute-start.8 = (bf16[2,2,2,64,256]{4,3,0,2,1:T(8,128)(2,1)}, bf16[2,2,2,64,256]{4,3,0,2,1:T(8,128)(2,1)}, u32[]{:S(2)}, u32[]{:S(2)}) collective-permute-start(bf16[2,2,2,64,256]{4,3,0,2,1:T(8,128)(2,1)} %fusion.89), channel_id=1, source_target_pairs={{0,2},{2,4},{4,6},{6,8},{8,10},{10,12},{12,14},{14,16},{16,18},{18... | collective-permute-start | bytes 786440 | tf_op jit(solution)/shard_map/ppermute | solution.py:22
  816.0 14.6 %collective-permute-start.14 = (bf16[2,2,2,64,256]{4,3,0,2,1:T(8,128)(2,1)}, bf16[2,2,2,64,256]{4,3,0,2,1:T(8,128)(2,1)S(1)}, u32[]{:S(2)}, u32[]{:S(2)}) collective-permute-start(bf16[2,2,2,64,256]{4,3,0,2,1:T(8,128)(2,1)} %fusion.89), channel_id=1, source_target_pairs={{0,254},{2,0},{4,2},{6,4},{8,6},{10,8},{12,10},{14,12},{16,14},{18... | collective-permute-start | bytes 786440 | tf_op jit(solution)/shard_map/ppermute | solution.py:22
  830.6 20.3 %collective-permute-start.11 = (bf16[2,2,2,64,256]{4,3,0,2,1:T(8,128)(2,1)}, bf16[2,2,2,64,256]{4,3,0,2,1:T(8,128)(2,1)S(1)}, u32[]{:S(2)}, u32[]{:S(2)}) collective-permute-start(bf16[2,2,2,64,256]{4,3,0,2,1:T(8,128)(2,1)} %collective-permute-done.8), channel_id=1, source_target_pairs={{0,2},{2,4},{4,6},{6,8},{8,10},{10,12},{12,14},{14,16},{16,18},{18... | collective-permute-start | bytes 786440 | tf_op jit(solution)/shard_map/ppermute | solution.py:22
  845.6 17.6 %collective-permute-start.17 = (bf16[2,2,2,64,256]{4,3,0,2,1:T(8,128)(2,1)S(1)}, bf16[2,2,2,64,256]{4,3,0,2,1:T(8,128)(2,1)S(1)}, u32[]{:S(2)}, u32[]{:S(2)}) collective-permute-start(bf16[2,2,2,64,256]{4,3,0,2,1:T(8,128)(2,1)S(1)} %collective-permute-done.14), channel_id=1, source_target_pairs={{0,254},{2,0},{4,2},{6,4},{8,6},{10,8},{12,10},{14,12},{16,14},{18... | collective-permute-start | bytes 786440 | tf_op jit(solution)/shard_map/ppermute | solution.py:22
  1014.4 10.3 collective-permute-start.23
  1024.7 17.5 %collective-permute-start.24 = (bf16[2,2,2,64,128]{4,3,0,2,1:T(8,128)(2,1)S(1)}, bf16[2,2,2,64,128]{4,3,0,2,1:T(8,128)(2,1)S(1)}, u32[]{:S(2)}, u32[]{:S(2)}) collective-permute-start(bf16[2,2,2,64,128]{4,3,0,2,1:T(8,128)(2,1)S(1)} %collective-permute-done.23), channel_id=1, source_target_pairs={{0,16},{16,0},{2,18},{18,2},{4,20},{20,4},{6,22},{22,6},{8,24},{24... | collective-permute-start | bytes 393224 | tf_op jit(solution)/shard_map/ppermute | solution.py:17
  1042.2 24.1 %collective-permute-start.25 = (bf16[2,2,2,64,128]{4,3,0,2,1:T(8,128)(2,1)S(1)}, bf16[2,2,2,64,128]{4,3,0,2,1:T(8,128)(2,1)S(1)}, u32[]{:S(2)}, u32[]{:S(2)}) collective-permute-start(bf16[2,2,2,64,128]{4,3,0,2,1:T(8,128)(2,1)S(1)} %collective-permute-done.24), channel_id=1, source_target_pairs={{0,32},{32,0},{2,34},{34,2},{4,36},{36,4},{6,38},{38,6},{8,40},{40... | collective-permute-start | bytes 393224 | tf_op jit(solution)/shard_map/ppermute | solution.py:17
  1073.2 8.4 collective-permute-start.27
  (65 other events, 1564.9 us)
Sparse Core Ops, SparseCore 0:
  901.9 92.3 reduce-scatter.3
where the time goes:
time: 1100 us; the launch traced here: 1090 us
  blocking collectives  583 us (53%)
  waiting for transfers between devices  201 us (18%)
  starting transfers between devices  120 us (11%)
  matrix products  76.2 us (7%)
  other arithmetic  56.5 us (5%)
  local copies, waits for them, and re-layouts  38.9 us (4%)
  between operations  15.1 us (1%)
    psum x1, blocking collectives, per_device(): spread = lax.psum(spread, ('ka', 'isdf'))  583 us
    ppermute x16, waiting for transfers between devices, swapped(): return lax.ppermute(block, axis, route)  108 us
    unnamed x2, waiting for transfers between devices  92.5 us
    ppermute x16, starting transfers between devices, swapped(): return lax.ppermute(block, axis, route)  71.8 us
    dot_general x48, matrix products, single(): jnp.einsum(pattern, first, second, preferred_element_type=jnp.float32)  53.3 us
    ppermute x12, starting transfers between devices, shifted(): lax.ppermute(value, axis, [(i, (i + by) % size) for i in range(size)])  47.7 us
    dot_general x10, matrix products, accumulate(): jnp.einsum('kw,wrmn->rkmn', selector[:, visitor], screened, preferred_ele...  22.4 us
  transfers between devices with their start and end apart: 29, of which 14 were waited for; matrix products, arithmetic and copies ran while one was open for 12% of the time, Pallas kernels for 0%

commit v1 on v0

--- a/solution.py
+++ b/solution.py
@@ -96,7 +96,8 @@
     )
     density = jnp.stack([rho_real, rho_imag], axis=1)
     spread = jnp.einsum("nm,brm->brn", coulomb, density, precision=HIGHEST)
-    spread = lax.psum(spread, ("ka", "isdf"))
+    for mesh_axis in ("isdf", "ka"):
+        spread = lax.psum(spread, mesh_axis)
     potential = lax.dynamic_slice_in_dim(spread, isdf_index * mu_count, mu_count, 2)
     class_ids = jnp.arange(screened.shape[0], dtype=jnp.int32)
 

time: 1100 us -> 703 us (0.64)
  blocking collectives: 583 us -> 221 us
  waiting for transfers between devices: 201 us -> 165 us
    psum x1 -> x2, blocking collectives: 583 us -> 221 us  [per_device(): spread = lax.psum(spread, mesh_axis)]
    unnamed x2, waiting for transfers between devices: 92.5 us -> 56.5 us
  transfers between devices with their start and end apart: 29 -> 29, of which waited for: 14 -> 14; matrix products, arithmetic and copies ran while one was open for 12% -> 19% of each run, Pallas kernels for 0% -> 0%
where the time goes in v1:
time: 703 us; the launch traced here: 693 us
  blocking collectives  221 us (31%)
  waiting for transfers between devices  165 us (23%)
  starting transfers between devices  120 us (17%)
  matrix products  76.2 us (11%)
  other arithmetic  56.4 us (8%)
  local copies, waits for them, and re-layouts  38.9 us (6%)
  between operations  15.1 us (2%)
    psum x2, blocking collectives, per_device(): spread = lax.psum(spread, mesh_axis)  221 us
    ppermute x16, waiting for transfers between devices, swapped(): return lax.ppermute(block, axis, route)  108 us
    ppermute x16, starting transfers between devices, swapped(): return lax.ppermute(block, axis, route)  71.8 us
    unnamed x2, waiting for transfers between devices  56.5 us
    dot_general x48, matrix products, single(): jnp.einsum(pattern, first, second, preferred_element_type=jnp.float32)  53.3 us
    ppermute x12, starting transfers between devices, shifted(): lax.ppermute(value, axis, [(i, (i + by) % size) for i in range(size)])  47.7 us
    dot_general x10, matrix products, accumulate(): jnp.einsum('kw,wrmn->rkmn', selector[:, visitor], screened, preferred_ele...  22.3 us
    mul x10, other arithmetic, accumulate(): screen_real * visit_real - screen_imag * visit_imag  21.6 us
  transfers between devices with their start and end apart: 29, of which 14 were waited for; matrix products, arithmetic and copies ran while one was open for 19% of the time, Pallas kernels for 0%

profile of v1, /device:TPU:2, one launch (start us, length us, event | category | flops | bytes accessed | tf_op | source)
XLA Modules:
  0.0 692.6 jit_solution(1709878176859799108)
XLA Ops:
  8.6 10.8 %collective-permute-start.15 = (bf16[2,2,256,256]{3,2,1,0:T(8,128)(2,1)}, bf16[2,2,256,256]{3,2,1,0:T(8,128)(2,1)}, u32[]{:S(2)}, u32[]{:S(2)}) collective-permute-start(bf16[2,2,256,256]{3,2,1,0:T(8,128)(2,1)} %param.9), channel_id=1, source_target_pairs={{0,254},{2,0},{4,2},{6,4},{8,6},{10,8},{12,10},{14,12},{16,14},{18... | collective-permute-start | bytes 1572872 | tf_op jit(solution)/shard_map/ppermute | solution.py:22
  21.3 5.8 collective-permute-start.16
  76.6 6.6 collective-permute-done.2
  87.2 12.3 %collective-permute-done.3 = bf16[2,2,2,64,256]{4,3,0,2,1:T(8,128)(2,1)S(1)} collective-permute-done((bf16[2,2,2,64,256]{4,3,0,2,1:T(8,128)(2,1)S(1)}, bf16[2,2,2,64,256]{4,3,0,2,1:T(8,128)(2,1)S(1)}, u32[]{:S(2)}, u32[]{:S(2)}) %collective-permute-start.3) | collective-permute-done | bytes 262176 | tf_op jit(solution)/shard_map/ppermute | solution.py:17
  103.9 22.7 %collective-permute-done.4 = bf16[2,2,2,64,256]{4,3,0,2,1:T(8,128)(2,1)S(1)} collective-permute-done((bf16[2,2,2,64,256]{4,3,0,2,1:T(8,128)(2,1)S(1)}, bf16[2,2,2,64,256]{4,3,0,2,1:T(8,128)(2,1)S(1)}, u32[]{:S(2)}, u32[]{:S(2)}) %collective-permute-start.4) | collective-permute-done | bytes 262176 | tf_op jit(solution)/shard_map/ppermute | solution.py:17
  126.6 14.7 %collective-permute-start.5 = (bf16[2,2,2,64,256]{4,3,0,2,1:T(8,128)(2,1)S(1)}, bf16[2,2,2,64,256]{4,3,0,2,1:T(8,128)(2,1)S(1)}, u32[]{:S(2)}, u32[]{:S(2)}) collective-permute-start(bf16[2,2,2,64,256]{4,3,0,2,1:T(8,128)(2,1)S(1)} %collective-permute-done.4), channel_id=1, source_target_pairs={{0,32},{32,0},{2,34},{34,2},{4,36},{36,4},{6,38},{38,6},{8,40},{40... | collective-permute-start | bytes 786440 | tf_op jit(solution)/shard_map/ppermute | solution.py:17
  143.3 14.9 %collective-permute-done.5 = bf16[2,2,2,64,256]{4,3,0,2,1:T(8,128)(2,1)S(1)} collective-permute-done((bf16[2,2,2,64,256]{4,3,0,2,1:T(8,128)(2,1)S(1)}, bf16[2,2,2,64,256]{4,3,0,2,1:T(8,128)(2,1)S(1)}, u32[]{:S(2)}, u32[]{:S(2)}) %collective-permute-start.5) | collective-permute-done | bytes 262176 | tf_op jit(solution)/shard_map/ppermute | solution.py:17
  163.0 5.4 collective-permute-done.6
  198.8 5.8 collective-permute-start.19
  206.5 5.8 collective-permute-start.18
  228.4 6.6 psum.14
  235.1 214.8 %psum.15 = f32[2,2,512]{2,1,0:T(2,128)S(1)} all-reduce(f32[2,2,512]{2,1,0:T(2,128)S(1)} %psum.14), channel_id=1, replica_groups=mesh['pm'=2,'ka'=128,'isdf'=2] {'ka'}, use_global_device_ids=true, to_apply=%region_1.2 | all-reduce | flops 2048 | bytes 16384 | tf_op jit(solution)/shard_map/psum | solution.py:100
  484.0 5.3 collective-permute-start.17
  517.0 9.2 %add_convert_fusion = bf16[2,2,256,512]{3,2,0,1:T(8,128)(2,1)S(1)} fusion(f32[2,256,512]{2,1,0:T(8,128)} %get-tuple-element.48, f32[2,256,512]{2,1,0:T(8,128)S(1)} %copy-done.14, f32[2,256,512]{2,1,0:T(8,128)} %get-tuple-element.69, f32[2,256,512]{2,1,0:T(8,128)S(1)} %copy-done.13, f32[2,256,512]{2,1,0:T(8,128)} %get-tuple-element.47, ...), kind=kLoop, calls=%fused_computation.2 | loop fusion | flops 20971520 | bytes 42991616 | tf_op jit(solution)/shard_map/convert_element_type | solution.py:152
  526.2 9.5 %add_convert_fusion.1 = bf16[2,2,256,512]{3,2,0,1:T(8,128)(2,1)S(1)} fusion(f32[2,256,512]{2,1,0:T(8,128)} %get-tuple-element.48, f32[2,256,512]{2,1,0:T(8,128)S(1)} %copy-done.14, f32[2,256,512]{2,1,0:T(8,128)} %get-tuple-element.69, f32[2,256,512]{2,1,0:T(8,128)S(1)} %copy-done.13, f32[2,256,512]{2,1,0:T(8,128)} %get-tuple-element.47, ...), kind=kLoop, calls=%fused_computation.3 | loop fusion | flops 20971520 | bytes 42991616 | tf_op jit(solution)/shard_map/convert_element_type | solution.py:151
  540.1 56.5 %reduce-scatter.4.cloned.1.call-done = bf16[128,512]{1,0:T(8,128)(2,1)} async-done(((bf16[256,512]{1,0:T(8,128)(2,1)}), bf16[128,512]{1,0:T(8,128)(2,1)}) %reduce-scatter.4.cloned.1.call-update) | async-done | bytes 131088
  601.4 4.6 collective-permute-done.20
  616.8 4.5 collective-permute-start.23
  621.2 5.9 collective-permute-done.23
  627.1 7.6 %collective-permute-start.24 = (bf16[2,2,2,64,128]{4,3,0,2,1:T(8,128)(2,1)S(1)}, bf16[2,2,2,64,128]{4,3,0,2,1:T(8,128)(2,1)S(1)}, u32[]{:S(2)}, u32[]{:S(2)}) collective-permute-start(bf16[2,2,2,64,128]{4,3,0,2,1:T(8,128)(2,1)S(1)} %collective-permute-done.23), channel_id=1, source_target_pairs={{0,16},{16,0},{2,18},{18,2},{4,20},{20,4},{6,22},{22,6},{8,24},{24... | collective-permute-start | bytes 393224 | tf_op jit(solution)/shard_map/ppermute | solution.py:17
  634.7 9.9 %collective-permute-done.24 = bf16[2,2,2,64,128]{4,3,0,2,1:T(8,128)(2,1)S(1)} collective-permute-done((bf16[2,2,2,64,128]{4,3,0,2,1:T(8,128)(2,1)S(1)}, bf16[2,2,2,64,128]{4,3,0,2,1:T(8,128)(2,1)S(1)}, u32[]{:S(2)}, u32[]{:S(2)}) %collective-permute-start.24) | collective-permute-done | bytes 131104 | tf_op jit(solution)/shard_map/ppermute | solution.py:17
  644.6 12.0 %collective-permute-start.25 = (bf16[2,2,2,64,128]{4,3,0,2,1:T(8,128)(2,1)S(1)}, bf16[2,2,2,64,128]{4,3,0,2,1:T(8,128)(2,1)S(1)}, u32[]{:S(2)}, u32[]{:S(2)}) collective-permute-start(bf16[2,2,2,64,128]{4,3,0,2,1:T(8,128)(2,1)S(1)} %collective-permute-done.24), channel_id=1, source_target_pairs={{0,32},{32,0},{2,34},{34,2},{4,36},{36,4},{6,38},{38,6},{8,40},{40... | collective-permute-start | bytes 393224 | tf_op jit(solution)/shard_map/ppermute | solution.py:17
  656.6 12.1 %collective-permute-done.25 = bf16[2,2,2,64,128]{4,3,0,2,1:T(8,128)(2,1)S(1)} collective-permute-done((bf16[2,2,2,64,128]{4,3,0,2,1:T(8,128)(2,1)S(1)}, bf16[2,2,2,64,128]{4,3,0,2,1:T(8,128)(2,1)S(1)}, u32[]{:S(2)}, u32[]{:S(2)}) %collective-permute-start.25) | collective-permute-done | bytes 131104 | tf_op jit(solution)/shard_map/ppermute | solution.py:17
  679.4 4.5 collective-permute-done.27
  (294 shorter events, 209.9 us)
Async XLA Ops:
  6.5 590.1 %reduce-scatter.4.cloned.1.call-start = ((), (), s32[]{:S(2)}) async-start(), calls=%async_computation.1 | async-start | bytes 393216
  6.5 198.0 %collective-permute-start.9 = (bf16[2,2,256,256]{3,2,1,0:T(8,128)(2,1)}, bf16[2,2,256,256]{3,2,1,0:T(8,128)(2,1)}, u32[]{:S(2)}, u32[]{:S(2)}) collective-permute-start(bf16[2,2,256,256]{3,2,1,0:T(8,128)(2,1)} %param.9), channel_id=1, source_target_pairs={{0,2},{2,4},{4,6},{6,8},{8,10},{10,12},{12,14},{14,16},{16,18},{18... | collective-permute-start | bytes 1572872 | tf_op jit(solution)/shard_map/ppermute | solution.py:22
  8.6 197.9 %collective-permute-start.15 = (bf16[2,2,256,256]{3,2,1,0:T(8,128)(2,1)}, bf16[2,2,256,256]{3,2,1,0:T(8,128)(2,1)}, u32[]{:S(2)}, u32[]{:S(2)}) collective-permute-start(bf16[2,2,256,256]{3,2,1,0:T(8,128)(2,1)} %param.9), channel_id=1, source_target_pairs={{0,254},{2,0},{4,2},{6,4},{8,6},{10,8},{12,10},{14,12},{16,14},{18... | collective-permute-start | bytes 1572872 | tf_op jit(solution)/shard_map/ppermute | solution.py:22
  19.4 177.3 %collective-permute-start.10 = (bf16[2,2,64,512]{3,2,1,0:T(8,128)(2,1)}, bf16[2,2,64,512]{3,2,1,0:T(8,128)(2,1)}, u32[]{:S(2)}, u32[]{:S(2)}) collective-permute-start(bf16[2,2,64,512]{3,2,1,0:T(8,128)(2,1)} %param.10), channel_id=1, source_target_pairs={{0,2},{2,4},{4,6},{6,8},{8,10},{10,12},{12,14},{14,16},{16,18},{18... | collective-permute-start | bytes 786440 | tf_op jit(solution)/shard_map/ppermute | solution.py:22
  21.3 177.4 %collective-permute-start.16 = (bf16[2,2,64,512]{3,2,1,0:T(8,128)(2,1)}, bf16[2,2,64,512]{3,2,1,0:T(8,128)(2,1)}, u32[]{:S(2)}, u32[]{:S(2)}) collective-permute-start(bf16[2,2,64,512]{3,2,1,0:T(8,128)(2,1)} %param.10), channel_id=1, source_target_pairs={{0,254},{2,0},{4,2},{6,4},{8,6},{10,8},{12,10},{14,12},{16,14},{18... | collective-permute-start | bytes 786440 | tf_op jit(solution)/shard_map/ppermute | solution.py:22
  28.1 40.2 %collective-permute-start = (bf16[2,2,2,64,256]{4,3,0,2,1:T(8,128)(2,1)S(1)}, bf16[2,2,2,64,256]{4,3,0,2,1:T(8,128)(2,1)S(1)}, u32[]{:S(2)}, u32[]{:S(2)}) collective-permute-start(bf16[2,2,2,64,256]{4,3,0,2,1:T(8,128)(2,1)S(1)} %bitcast.651), channel_id=1, source_target_pairs={{0,256},{256,0},{1,257},{257,1},{2,258},{258,2},{3,259},{259,3},{4... | collective-permute-start | bytes 786440 | tf_op jit(solution)/shard_map/ppermute | solution.py:17
  72.5 10.7 %collective-permute-start.2 = (bf16[2,2,2,64,256]{4,3,0,2,1:T(8,128)(2,1)S(1)}, bf16[2,2,2,64,256]{4,3,0,2,1:T(8,128)(2,1)S(1)}, u32[]{:S(2)}, u32[]{:S(2)}) collective-permute-start(bf16[2,2,2,64,256]{4,3,0,2,1:T(8,128)(2,1)S(1)} %collective-permute-done.1), channel_id=1, source_target_pairs={{0,4},{4,0},{2,6},{6,2},{8,12},{12,8},{10,14},{14,10},{16,20},{20,... | collective-permute-start | bytes 786440 | tf_op jit(solution)/shard_map/ppermute | solution.py:17
  83.2 16.3 %collective-permute-start.3 = (bf16[2,2,2,64,256]{4,3,0,2,1:T(8,128)(2,1)S(1)}, bf16[2,2,2,64,256]{4,3,0,2,1:T(8,128)(2,1)S(1)}, u32[]{:S(2)}, u32[]{:S(2)}) collective-permute-start(bf16[2,2,2,64,256]{4,3,0,2,1:T(8,128)(2,1)S(1)} %collective-permute-done.2), channel_id=1, source_target_pairs={{0,8},{8,0},{2,10},{10,2},{4,12},{12,4},{6,14},{14,6},{16,24},{24,... | collective-permute-start | bytes 786440 | tf_op jit(solution)/shard_map/ppermute | solution.py:17
  99.5 27.1 %collective-permute-start.4 = (bf16[2,2,2,64,256]{4,3,0,2,1:T(8,128)(2,1)S(1)}, bf16[2,2,2,64,256]{4,3,0,2,1:T(8,128)(2,1)S(1)}, u32[]{:S(2)}, u32[]{:S(2)}) collective-permute-start(bf16[2,2,2,64,256]{4,3,0,2,1:T(8,128)(2,1)S(1)} %collective-permute-done.3), channel_id=1, source_target_pairs={{0,16},{16,0},{2,18},{18,2},{4,20},{20,4},{6,22},{22,6},{8,24},{24... | collective-permute-start | bytes 786440 | tf_op jit(solution)/shard_map/ppermute | solution.py:17
  126.6 31.6 %collective-permute-start.5 = (bf16[2,2,2,64,256]{4,3,0,2,1:T(8,128)(2,1)S(1)}, bf16[2,2,2,64,256]{4,3,0,2,1:T(8,128)(2,1)S(1)}, u32[]{:S(2)}, u32[]{:S(2)}) collective-permute-start(bf16[2,2,2,64,256]{4,3,0,2,1:T(8,128)(2,1)S(1)} %collective-permute-done.4), channel_id=1, source_target_pairs={{0,32},{32,0},{2,34},{34,2},{4,36},{36,4},{6,38},{38,6},{8,40},{40... | collective-permute-start | bytes 786440 | tf_op jit(solution)/shard_map/ppermute | solution.py:17
  158.2 10.2 %collective-permute-start.6 = (bf16[2,2,2,64,256]{4,3,0,2,1:T(8,128)(2,1)S(1)}, bf16[2,2,2,64,256]{4,3,0,2,1:T(8,128)(2,1)}, u32[]{:S(2)}, u32[]{:S(2)}) collective-permute-start(bf16[2,2,2,64,256]{4,3,0,2,1:T(8,128)(2,1)S(1)} %collective-permute-done.5), channel_id=1, source_target_pairs={{0,64},{64,0},{2,66},{66,2},{4,68},{68,4},{6,70},{70,6},{8,72},{72... | collective-permute-start | bytes 786440 | tf_op jit(solution)/shard_map/ppermute | solution.py:17
  168.4 43.8 %collective-permute-start.7 = (bf16[2,2,2,64,256]{4,3,0,2,1:T(8,128)(2,1)}, bf16[2,2,2,64,256]{4,3,0,2,1:T(8,128)(2,1)}, u32[]{:S(2)}, u32[]{:S(2)}) collective-permute-start(bf16[2,2,2,64,256]{4,3,0,2,1:T(8,128)(2,1)} %collective-permute-done.6), channel_id=1, source_target_pairs={{0,128},{128,0},{2,130},{130,2},{4,132},{132,4},{6,134},{134,6},{8... | collective-permute-start | bytes 786440 | tf_op jit(solution)/shard_map/ppermute | solution.py:17
  196.7 297.1 %collective-permute-start.13 = (bf16[2,2,64,512]{3,2,1,0:T(8,128)(2,1)}, bf16[2,2,64,512]{3,2,1,0:T(8,128)(2,1)}, u32[]{:S(2)}, u32[]{:S(2)}) collective-permute-start(bf16[2,2,64,512]{3,2,1,0:T(8,128)(2,1)} %collective-permute-done.10), channel_id=1, source_target_pairs={{0,2},{2,4},{4,6},{6,8},{8,10},{10,12},{12,14},{14,16},{16,18},{18... | collective-permute-start | bytes 786440 | tf_op jit(solution)/shard_map/ppermute | solution.py:22
  198.8 307.6 %collective-permute-start.19 = (bf16[2,2,64,512]{3,2,1,0:T(8,128)(2,1)}, bf16[2,2,64,512]{3,2,1,0:T(8,128)(2,1)}, u32[]{:S(2)}, u32[]{:S(2)}) collective-permute-start(bf16[2,2,64,512]{3,2,1,0:T(8,128)(2,1)} %collective-permute-done.16), channel_id=1, source_target_pairs={{0,254},{2,0},{4,2},{6,4},{8,6},{10,8},{12,10},{14,12},{16,14},{18... | collective-permute-start | bytes 786440 | tf_op jit(solution)/shard_map/ppermute | solution.py:22
  204.5 279.5 %collective-permute-start.12 = (bf16[2,2,256,256]{3,2,1,0:T(8,128)(2,1)}, bf16[2,2,256,256]{3,2,1,0:T(8,128)(2,1)}, u32[]{:S(2)}, u32[]{:S(2)}) collective-permute-start(bf16[2,2,256,256]{3,2,1,0:T(8,128)(2,1)} %collective-permute-done.9), channel_id=1, source_target_pairs={{0,2},{2,4},{4,6},{6,8},{8,10},{10,12},{12,14},{14,16},{16,18},{18... | collective-permute-start | bytes 1572872 | tf_op jit(solution)/shard_map/ppermute | solution.py:22
  206.5 295.2 %collective-permute-start.18 = (bf16[2,2,256,256]{3,2,1,0:T(8,128)(2,1)}, bf16[2,2,256,256]{3,2,1,0:T(8,128)(2,1)}, u32[]{:S(2)}, u32[]{:S(2)}) collective-permute-start(bf16[2,2,256,256]{3,2,1,0:T(8,128)(2,1)} %collective-permute-done.15), channel_id=1, source_target_pairs={{0,254},{2,0},{4,2},{6,4},{8,6},{10,8},{12,10},{14,12},{16,14},{18... | collective-permute-start | bytes 1572872 | tf_op jit(solution)/shard_map/ppermute | solution.py:22
  221.3 233.1 %collective-permute-start.8 = (bf16[2,2,2,64,256]{4,3,0,2,1:T(8,128)(2,1)}, bf16[2,2,2,64,256]{4,3,0,2,1:T(8,128)(2,1)}, u32[]{:S(2)}, u32[]{:S(2)}) collective-permute-start(bf16[2,2,2,64,256]{4,3,0,2,1:T(8,128)(2,1)} %fusion.89), channel_id=1, source_target_pairs={{0,2},{2,4},{4,6},{6,8},{8,10},{10,12},{12,14},{14,16},{16,18},{18... | collective-permute-start | bytes 786440 | tf_op jit(solution)/shard_map/ppermute | solution.py:22
  454.4 14.6 %collective-permute-start.14 = (bf16[2,2,2,64,256]{4,3,0,2,1:T(8,128)(2,1)}, bf16[2,2,2,64,256]{4,3,0,2,1:T(8,128)(2,1)S(1)}, u32[]{:S(2)}, u32[]{:S(2)}) collective-permute-start(bf16[2,2,2,64,256]{4,3,0,2,1:T(8,128)(2,1)} %fusion.89), channel_id=1, source_target_pairs={{0,254},{2,0},{4,2},{6,4},{8,6},{10,8},{12,10},{14,12},{16,14},{18... | collective-permute-start | bytes 786440 | tf_op jit(solution)/shard_map/ppermute | solution.py:22
  469.0 20.3 %collective-permute-start.11 = (bf16[2,2,2,64,256]{4,3,0,2,1:T(8,128)(2,1)}, bf16[2,2,2,64,256]{4,3,0,2,1:T(8,128)(2,1)S(1)}, u32[]{:S(2)}, u32[]{:S(2)}) collective-permute-start(bf16[2,2,2,64,256]{4,3,0,2,1:T(8,128)(2,1)} %collective-permute-done.8), channel_id=1, source_target_pairs={{0,2},{2,4},{4,6},{6,8},{8,10},{10,12},{12,14},{14,16},{16,18},{18... | collective-permute-start | bytes 786440 | tf_op jit(solution)/shard_map/ppermute | solution.py:22
  484.0 17.6 %collective-permute-start.17 = (bf16[2,2,2,64,256]{4,3,0,2,1:T(8,128)(2,1)S(1)}, bf16[2,2,2,64,256]{4,3,0,2,1:T(8,128)(2,1)S(1)}, u32[]{:S(2)}, u32[]{:S(2)}) collective-permute-start(bf16[2,2,2,64,256]{4,3,0,2,1:T(8,128)(2,1)S(1)} %collective-permute-done.14), channel_id=1, source_target_pairs={{0,254},{2,0},{4,2},{6,4},{8,6},{10,8},{12,10},{14,12},{16,14},{18... | collective-permute-start | bytes 786440 | tf_op jit(solution)/shard_map/ppermute | solution.py:22
  616.8 10.3 %collective-permute-start.23 = (bf16[2,2,2,64,128]{4,3,0,2,1:T(8,128)(2,1)S(1)}, bf16[2,2,2,64,128]{4,3,0,2,1:T(8,128)(2,1)S(1)}, u32[]{:S(2)}, u32[]{:S(2)}) collective-permute-start(bf16[2,2,2,64,128]{4,3,0,2,1:T(8,128)(2,1)S(1)} %collective-permute-done.22), channel_id=1, source_target_pairs={{0,8},{8,0},{2,10},{10,2},{4,12},{12,4},{6,14},{14,6},{16,24},{24,... | collective-permute-start | bytes 393224 | tf_op jit(solution)/shard_map/ppermute | solution.py:17
  627.1 17.5 %collective-permute-start.24 = (bf16[2,2,2,64,128]{4,3,0,2,1:T(8,128)(2,1)S(1)}, bf16[2,2,2,64,128]{4,3,0,2,1:T(8,128)(2,1)S(1)}, u32[]{:S(2)}, u32[]{:S(2)}) collective-permute-start(bf16[2,2,2,64,128]{4,3,0,2,1:T(8,128)(2,1)S(1)} %collective-permute-done.23), channel_id=1, source_target_pairs={{0,16},{16,0},{2,18},{18,2},{4,20},{20,4},{6,22},{22,6},{8,24},{24... | collective-permute-start | bytes 393224 | tf_op jit(solution)/shard_map/ppermute | solution.py:17
  644.6 24.1 %collective-permute-start.25 = (bf16[2,2,2,64,128]{4,3,0,2,1:T(8,128)(2,1)S(1)}, bf16[2,2,2,64,128]{4,3,0,2,1:T(8,128)(2,1)S(1)}, u32[]{:S(2)}, u32[]{:S(2)}) collective-permute-start(bf16[2,2,2,64,128]{4,3,0,2,1:T(8,128)(2,1)S(1)} %collective-permute-done.24), channel_id=1, source_target_pairs={{0,32},{32,0},{2,34},{34,2},{4,36},{36,4},{6,38},{38,6},{8,40},{40... | collective-permute-start | bytes 393224 | tf_op jit(solution)/shard_map/ppermute | solution.py:17
  675.5 8.4 %collective-permute-start.27 = (bf16[2,2,2,64,128]{4,3,0,2,1:T(8,128)(2,1)S(1)}, bf16[2,2,2,64,128]{4,3,0,2,1:T(8,128)(2,1)S(1)}, u32[]{:S(2)}, u32[]{:S(2)}) collective-permute-start(bf16[2,2,2,64,128]{4,3,0,2,1:T(8,128)(2,1)S(1)} %collective-permute-done.26), channel_id=1, source_target_pairs={{0,128},{128,0},{2,130},{130,2},{4,132},{132,4},{6,134},{134,6},{8... | collective-permute-start | bytes 393224 | tf_op jit(solution)/shard_map/ppermute | solution.py:17
  (65 other events, 1131.2 us)
Sparse Core Ops, SparseCore 0:
  540.2 56.3 reduce-scatter.3
